TPU v7x, 32 devices: a whole 2x2x4 slice. The times are simulated.
32 devices in a mesh: level: 16 (over z, y, core), band: 2 (over x).
Axes of the slice: x: 2, y: 2, z: 4, core: 2. Of those that a mesh axis runs over, the one named last changes fastest.
Arguments:
- latents: float32 [16, 4, 10, 64], P('level', None, 'band'), may hold values from -18 to 18
- timesteps: int32 [16], P('level'), may hold values from 16 to 999
- fresh: float32 [1, 4, 10, 64], P(None, None, 'band'), may hold values from -6 to 6
- w_in: float32 [4, 320], replicated, may hold values from -3 to 3
- conv_first: float32 [3, 3, 320, 320], replicated, may hold values from -0.109375 to 0.109375
- conv_second: float32 [3, 3, 320, 320], replicated, may hold values from -0.109375 to 0.109375
- w_time: float32 [320, 320], replicated, may hold values from -0.3125 to 0.3125
- temporal: float32 [3, 320, 320], replicated, may hold values from -0.1875 to 0.1875
- w_out: float32 [320, 4], replicated, may hold values from -0.3125 to 0.3125
Outputs:
- queue: float32 [16, 4, 10, 64], P('level', None, 'band')
All inputs are finite; a program needn't handle non-finite values.
Results may differ from a plain program's by a relative error of at most 0.0001.
Values sent between devices are 32-bit elements; how exact they have to be, the bound alone decides.
A program may use at most 128 MiB of HBM per device.

v0:
```python
import functools
import math

import jax
import jax.numpy as jnp
from jax import lax
from jax.experimental import pallas as pl
from jax.experimental.pallas import tpu as pltpu
from jax.sharding import PartitionSpec as P

GROUPS = 32
ITERS = 2
NSTEPS = 1000
STRIDE = 16
EPSILON = 1e-05

MESH = pl.DeviceIdType.MESH
F32 = jnp.float32
BF16 = jnp.bfloat16
NN = (((1,), (0,)), ((), ()))
NT = (((1,), (1,)), ((), ()))
TN = (((0,), (0,)), ((), ()))


def dot(a, b, dims=NN):
    return lax.dot_general(a, b, dims, preferred_element_type=F32)


def split(v):
    high = v.astype(BF16)
    return high, (v - high.astype(F32)).astype(BF16)


def dot3(a, b, dims=NN):
    ah, al = split(a)
    bh, bl = split(b)
    return dot(ah, bh, dims) + dot(al, bh, dims) + dot(ah, bl, dims)


def silu(v):
    half = 0.5 * v
    return half + half * jnp.tanh(half)


def plan_at(step):
    rows = -(-NSTEPS // 1024) * 8
    position = lax.broadcasted_iota(jnp.int32, (rows, 128), 0) * 128
    position = position + lax.broadcasted_iota(jnp.int32, (rows, 128), 1)
    root_beta = math.sqrt(0.00085) + position.astype(F32) / (NSTEPS - 1) * (
        math.sqrt(0.012) - math.sqrt(0.00085)
    )
    kept = jnp.where(position <= step, 1.0 - root_beta * root_beta, 1.0)
    for axis, length in ((0, rows), (1, 128)):
        shift = length // 2
        while shift:
            kept = kept * pltpu.roll(kept, shift, axis)
            shift //= 2
    return kept[0:1, 0:1]


def pack_weights(raw, high_ref, low_ref, channels):
    rest = channels - 256
    high_ref[:, 3 * channels :, :] = jnp.zeros((4, 1024 - 3 * channels, 256), BF16)
    low_ref[:, 3 * channels :, :] = jnp.zeros((4, 1024 - 3 * channels, 256), BF16)
    for b in range(3):
        for n in range(4):
            if n < 3:
                piece = raw[n, b, :, 0:256]
            else:
                piece = jnp.concatenate(
                    [raw[a, b, :, 256:channels] for a in range(3)]
                    + [jnp.zeros((channels, 256 - 3 * rest), F32)],
                    axis=1,
                )
            high, low = split(piece)
            start = 768 + b * rest
            high_ref[n, b * 256 : (b + 1) * 256, :] = high[0:256]
            low_ref[n, b * 256 : (b + 1) * 256, :] = low[0:256]
            high_ref[n, start : start + rest, :] = high[256:channels]
            low_ref[n, start : start + rest, :] = low[256:channels]


def kernel(
    sizes,
    step_ref,
    pack_ref,
    small_ref,
    conv_first_hbm,
    conv_second_hbm,
    w_time_hbm,
    temporal_hbm,
    out_ref,
    raw_first,
    raw_second,
    raw_time,
    raw_temporal,
    first_high,
    first_low,
    second_high,
    second_low,
    act_high,
    act_low,
    lifted_ref,
    value_ref,
    rest_ref,
    gathered,
    send_frame,
    recv_frame,
    send_tap,
    recv_tap,
    send_last,
    recv_last,
    load_sem,
    band_send,
    band_recv,
    level_send,
    level_recv,
):
    n_level, n_band, channels, height, width, chunk = sizes
    rest = channels - 256
    pixels = height * width
    held = pixels // n_band
    block = chunk * width
    level = lax.axis_index("level")
    band = lax.axis_index("band")

    loads = [
        pltpu.make_async_copy(source, target, load_sem.at[i])
        for i, (source, target) in enumerate(
            (
                (conv_first_hbm, raw_first),
                (w_time_hbm, raw_time),
                (temporal_hbm, raw_temporal),
                (conv_second_hbm, raw_second),
            )
        )
    ]
    for load in loads:
        load.start()

    recv_frame[...] = jnp.zeros_like(recv_frame)
    recv_tap[...] = jnp.zeros_like(recv_tap)
    recv_last[...] = jnp.zeros_like(recv_last)

    has_up = level + 1 < n_level
    has_two_up = level + 2 < n_level
    has_down = level >= 1
    has_two_down = level >= 2

    barrier = pltpu.get_barrier_semaphore()
    peers = [lax.rem(band + i, n_band) for i in range(1, n_band)]

    def greet(who):
        pl.semaphore_signal(barrier, inc=1, device_id=who, device_id_type=MESH)

    for peer in peers:
        greet({"band": peer})
    pl.when(has_down)(lambda: greet({"level": level - 1}))
    pl.when(has_two_down)(lambda: greet({"level": level - 2}))
    pl.when(has_up)(lambda: greet({"level": level + 1}))
    expected = n_band - 1
    for there in (has_up, has_two_up, has_down):
        expected = expected + jnp.where(there, 1, 0)
    pl.semaphore_wait(barrier, expected)

    def band_copy(i):
        return pltpu.make_async_remote_copy(
            src_ref=pack_ref,
            dst_ref=gathered.at[i],
            send_sem=band_send.at[i],
            recv_sem=band_recv.at[i],
            device_id={"band": peers[i]},
            device_id_type=MESH,
        )

    for i in range(n_band - 1):
        band_copy(i).start()

    w_in = small_ref[0:8, :]
    w_out = small_ref[8:16, :]

    per_group = channels // GROUPS
    def group_of(axis):
        index = lax.broadcasted_iota(jnp.int32, (channels, channels), axis).astype(F32)
        return jnp.floor((index + 0.5) * (1.0 / per_group))
    same_group = jnp.where(group_of(0) == group_of(1), 1.0, 0.0).astype(BF16)

    step = step_ref[0]
    alpha_now = plan_at(step)
    alpha_prev = plan_at(step - STRIDE)
    scale_x = jnp.sqrt(alpha_prev) / jnp.sqrt(alpha_now)
    scale_noise = jnp.sqrt(1.0 - alpha_prev) - scale_x * jnp.sqrt(1.0 - alpha_now)

    lane = lax.broadcasted_iota(jnp.int32, (8, channels), 1)
    half_width = channels // 2
    harmonic_index = jnp.where(lane < half_width, lane, lane - half_width).astype(F32)
    frequency = jnp.exp(-math.log(10000.0) * harmonic_index / half_width)
    angle = step.astype(F32) * frequency
    harmonic = jnp.where(lane < half_width, jnp.cos(angle), jnp.sin(angle))

    loads[0].wait()
    pack_weights(raw_first, first_high, first_low, channels)
    loads[1].wait()
    embedded = silu(dot3(harmonic, raw_time[...]))[0:1, :]
    loads[2].wait()
    folded = jnp.concatenate(
        [dot3(w_out, raw_temporal[k], NT) for k in range(3)]
        + [jnp.zeros((8, channels), F32)],
        axis=0,
    )
    folded_high, folded_low = split(folded)
    w_out_high, w_out_low = split(
        jnp.concatenate([w_out, jnp.zeros((24, channels), F32)], axis=0)
    )
    loads[3].wait()
    pack_weights(raw_second, second_high, second_low, channels)

    border = jnp.zeros((width, 1024), BF16)
    for ref in (act_high, act_low):
        ref[0:width, :] = border
        ref[width + pixels :, :] = border
    rest_ref[0:width, :] = jnp.zeros((width, 256), F32)
    rest_ref[width + pixels :, :] = jnp.zeros((width, 256), F32)

    for i in range(n_band - 1):
        band_copy(i).wait()

    def from_band(j):
        found = pack_ref[...]
        for i in range(n_band - 1):
            found = jnp.where(lax.rem(band - i - 1 + n_band, n_band) == j, gathered[i], found)
        return found

    packs = [from_band(j) for j in range(n_band)]
    frame = jnp.concatenate([p[0:8] for p in packs], axis=1)
    entering = jnp.concatenate([p[8:16] for p in packs], axis=1)

    def norm_terms(ref):
        def add(i, sums):
            part = ref[pl.ds(pl.multiple_of(i * block, block), block), :]
            return (
                sums[0] + jnp.sum(part, axis=0, keepdims=True),
                sums[1] + jnp.sum(part * part, axis=0, keepdims=True),
            )

        zero = jnp.zeros((1, channels), F32)
        sums = lax.fori_loop(0, height // chunk, add, (zero, zero))
        row = lax.broadcasted_iota(jnp.int32, (16, channels), 0)
        stacked = jnp.zeros((16, channels), F32)
        for which, left in enumerate(sums):
            for part in range(3):
                piece = left.astype(BF16).astype(F32)
                left = left - piece
                stacked = jnp.where(row == which * 3 + part, piece, stacked)
        totals = dot(stacked.astype(BF16), same_group)
        members = float(pixels * per_group)
        center = (totals[0:1] + totals[1:2] + totals[2:3]) / members
        square = (totals[3:4] + totals[4:5] + totals[5:6]) / members
        return center, lax.rsqrt(square - center * center + EPSILON)

    column = lax.broadcasted_iota(jnp.int32, (width, channels), 0)

    def fill_act(ref, terms):
        center, factor = terms

        def one_row(i, carry):
            v = silu((ref[pl.ds(pl.multiple_of(i * width, width), width), :] - center) * factor)
            before = jnp.where(column == 0, 0.0, pltpu.roll(v, 1, 0))
            after = jnp.where(column == width - 1, 0.0, pltpu.roll(v, width - 1, 0))
            taps = (before, v, after)
            wide = jnp.concatenate(
                [t[:, 0:256] for t in taps]
                + [t[:, 256:channels] for t in taps]
                + [jnp.zeros((width, 1024 - 3 * channels), F32)],
                axis=1,
            )
            high, low = split(wide)
            place = pl.ds(pl.multiple_of((i + 1) * width, width), width)
            act_high[place, :] = high
            act_low[place, :] = low
            return carry

        lax.fori_loop(0, height, one_row, 0)

    def convolve(high_ref, low_ref, add):
        def product(start, n):
            place = pl.ds(pl.multiple_of(start, width), block)
            left = act_high[place, :]
            return (
                dot(left, high_ref[n])
                + dot(act_low[place, :], high_ref[n])
                + dot(left, low_ref[n])
            )

        def part(i, carry):
            base = i * block
            rest_ref[pl.ds(pl.multiple_of(base + width, width), block), :] = product(
                base + width, 3
            )
            total = product(base, 0) + product(base + width, 1)
            total = total + product(base + 2 * width, 2)
            place = pl.ds(pl.multiple_of(base, width), block)
            value_ref[place, 0:256] = total + add(place)[:, 0:256]
            return carry

        lax.fori_loop(0, height // chunk, part, 0)

        def end(i, carry):
            base = i * width
            total = add(pl.ds(pl.multiple_of(base, width), width))[:, 256:channels]
            for a in range(3):
                rows = pl.ds(pl.multiple_of(base + a * width, width), width)
                total = total + rest_ref[rows, a * rest : (a + 1) * rest]
            value_ref[pl.ds(pl.multiple_of(base, width), width), 256:channels] = total
            return carry

        lax.fori_loop(0, height, end, 0)

    def project(high, low, values):
        vh, vl = split(values)
        both = dot(jnp.concatenate([high, low], axis=0), vh, NT)
        return both[0:32] + both[32:64] + dot(high, vl, NT)

    def level_copy(i, source, target, to):
        return pltpu.make_async_remote_copy(
            src_ref=source,
            dst_ref=target,
            send_sem=level_send.at[i],
            recv_sem=level_recv.at[i],
            device_id={"level": to},
            device_id_type=MESH,
        )

    def run_block(frame):
        lifted_ref[...] = lax.dot_general(
            frame.T, w_in, NN, precision=lax.Precision.HIGHEST, preferred_element_type=F32
        )
        fill_act(lifted_ref, norm_terms(lifted_ref))
        convolve(first_high, first_low, lambda place: embedded)
        fill_act(value_ref, norm_terms(value_ref))
        convolve(second_high, second_low, lambda place: lifted_ref[place, :])
        return norm_terms(value_ref)

    center, factor = run_block(frame)
    hidden = value_ref[...]
    taps = project(folded_high, folded_low, silu((hidden - center) * factor))
    local = project(w_out_high, w_out_low, hidden)[0:8] + taps[8:16]
    send_frame[0:8, :] = scale_x * frame + scale_noise * local
    send_frame[8:16, :] = jnp.broadcast_to(scale_noise, (8, pixels))
    send_tap[...] = taps[0:8]
    frame_copy = level_copy(0, send_frame, recv_frame, level + 1)
    tap_copy = level_copy(1, send_tap, recv_tap, level + 2)
    pl.when(has_two_up)(lambda: tap_copy.start())
    pl.when(has_up)(lambda: frame_copy.start())
    pl.when(has_two_down)(lambda: tap_copy.wait_recv())
    pl.when(has_down)(lambda: frame_copy.wait_recv())
    moved = recv_frame[0:8, :] + recv_frame[8:16, :] * (recv_tap[...] + taps[16:24])
    frame = jnp.where(level == 0, entering, moved)
    pl.when(has_two_up)(lambda: tap_copy.wait_send())
    pl.when(has_up)(lambda: frame_copy.wait_send())

    center, factor = run_block(frame)
    hidden = value_ref[pl.ds(pl.multiple_of(band * held, width), held), :]
    taps = project(folded_high, folded_low, silu((hidden - center) * factor))
    send_last[0] = taps[0:8]
    send_last[1] = taps[16:24]
    up_copy = level_copy(2, send_last.at[0], recv_last.at[0], level + 1)
    down_copy = level_copy(3, send_last.at[1], recv_last.at[1], level - 1)
    pl.when(has_up)(lambda: up_copy.start())
    pl.when(has_down)(lambda: down_copy.start())
    local = project(w_out_high, w_out_low, hidden)[0:8] + taps[8:16]
    mine = frame[:, 0:held]
    for j in range(1, n_band):
        mine = jnp.where(band == j, frame[:, j * held : (j + 1) * held], mine)
    pl.when(has_down)(lambda: up_copy.wait_recv())
    pl.when(has_up)(lambda: down_copy.wait_recv())
    out_ref[...] = scale_x * mine + scale_noise * (local + recv_last[0] + recv_last[1])
    pl.when(has_up)(lambda: up_copy.wait_send())
    pl.when(has_down)(lambda: down_copy.wait_send())


def on_device(
    mesh_sizes, latents, timesteps, fresh, w_in, conv_first, conv_second, w_time, temporal, w_out
):
    n_level, n_band = mesh_sizes
    lat, band_rows, width = latents.shape[1:]
    channels = w_in.shape[1]
    height = band_rows * n_band
    pixels = height * width
    held = band_rows * width
    chunk = max(d for d in range(1, 11) if height % d == 0)

    def eight(rows):
        return jnp.pad(rows, ((0, 8 - lat), (0, 0)))

    pack = jnp.concatenate(
        [eight(latents[0].reshape(lat, held)), eight(fresh[0].reshape(lat, held))], axis=0
    )
    small = jnp.concatenate([eight(w_in), eight(w_out.T)], axis=0)

    vmem = pl.BlockSpec(memory_space=pltpu.VMEM)
    hbm = pl.BlockSpec(memory_space=pl.ANY)
    sem = pltpu.SemaphoreType.DMA
    result = pl.pallas_call(
        functools.partial(kernel, (n_level, n_band, channels, height, width, chunk)),
        out_shape=jax.ShapeDtypeStruct((8, held), F32),
        in_specs=[pl.BlockSpec(memory_space=pltpu.SMEM), vmem, vmem, hbm, hbm, hbm, hbm],
        out_specs=vmem,
        scratch_shapes=[
            pltpu.VMEM(conv_first.shape, F32),
            pltpu.VMEM(conv_second.shape, F32),
            pltpu.VMEM(w_time.shape, F32),
            pltpu.VMEM(temporal.shape, F32),
            *[pltpu.VMEM((4, 1024, 256), BF16)] * 4,
            *[pltpu.VMEM((pixels + 2 * width, 1024), BF16)] * 2,
            *[pltpu.VMEM((pixels, channels), F32)] * 2,
            pltpu.VMEM((pixels + 2 * width, 256), F32),
            pltpu.VMEM((max(n_band - 1, 1), 16, held), F32),
            *[pltpu.VMEM((16, pixels), F32)] * 2,
            *[pltpu.VMEM((8, pixels), F32)] * 2,
            *[pltpu.VMEM((2, 8, held), F32)] * 2,
            sem((4,)),
            sem((max(n_band - 1, 1),)),
            sem((max(n_band - 1, 1),)),
            sem((4,)),
            sem((4,)),
        ],
        compiler_params=pltpu.CompilerParams(
            collective_id=0, has_side_effects=True, vmem_limit_bytes=60 * 1024 * 1024
        ),
    )(timesteps, pack, small, conv_first, conv_second, w_time, temporal)
    return result[0:lat].reshape(1, lat, band_rows, width)


def solution(mesh):
    placed = (
        P("level", None, "band", None),
        P("level"),
        P(None, None, "band", None),
        P(),
        P(),
        P(),
        P(),
        P(),
        P(),
    )
    return jax.shard_map(
        functools.partial(on_device, (mesh.shape["level"], mesh.shape["band"])),
        mesh=mesh,
        in_specs=placed,
        out_specs=P("level", None, "band", None),
        check_vma=False,
    )
```

profile of v0, /device:TPU:23, one launch (start us, length us, event | category | flops | bytes accessed | tf_op | source)
XLA Modules:
  0.0 62.2 jit_solution(16606782915037802327)
XLA Ops:
  0.0 0.7 %copy.13 = f32[1,4,5,64]{3,2,1,0:T(8,128)S(1)} copy(f32[1,4,5,64]{3,1,2,0:T(4,128)} %param.9) | data formatting | bytes 10240 | tf_op args[0]
  0.7 0.1 reshape_squeeze.6
  0.8 0.7 %copy.14 = f32[1,4,5,64]{3,2,1,0:T(8,128)S(1)} copy(f32[1,4,5,64]{3,1,2,0:T(4,128)} %param.11) | data formatting | bytes 10240 | tf_op args[2]
  1.5 0.1 reshape_squeeze.7
  1.6 1.3 %select_maximum_fusion = (f32[16,320]{1,0:T(8,128)}, f32[16,320]{1,0:T(8,128)}) fusion(f32[4,320]{1,0:T(4,128)} %bitcast.1, f32[4,320]{1,0:T(4,128)} %param.12, f32[4,320]{1,0:T(4,128)S(1)} %reshape_squeeze.7, f32[4,320]{1,0:T(4,128)S(1)} %reshape_squeeze.6), kind=kLoop, calls=%fused_computation | loop fusion | flops 40960 | bytes 61440 | tf_op jit(solution)/shard_map/concatenate | solution.py:399
  3.5 57.2 %shard_map.91 = f32[8,320]{1,0:T(8,128)} custom-call(s32[1]{0:T(128)S(6)} %copy.16.step_ref, f32[16,320]{1,0:T(8,128)} %get-tuple-element.6.pack_ref, f32[16,320]{1,0:T(8,128)} %get-tuple-element.5.small_ref, f32[3,3,320,320]{3,2,1,0:T(8,128)} %conv_first_hbm.1, f32[3,3,320,320]{3,2,1,0:T(8,128)} %conv_second_hbm.1, f32[320,320]{1,0:T(8,128)} %w_time_hbm.1, ...), custom_call_target="tpu_custom_call" | custom-call | tf_op jit(solution)/shard_map/pallas_call | solution.py:404
  60.8 0.7 %slice.3 = f32[4,320]{1,0:T(4,128)S(1)} slice(f32[8,320]{1,0:T(8,128)} %shard_map.91), slice={[0:4], [0:320]} | slice | bytes 10240 | tf_op jit(solution)/shard_map/slice | solution.py:432
  61.5 0.1 reshape.3
  61.6 0.6 copy.15
where the time goes:
time: 62.6 us; the launch traced here: 62.2 us
  Pallas kernels  57.2 us (91%)
  local copies, waits for them, and re-layouts  2.96 us (5%)
  other arithmetic  1.33 us (2%)
  between operations  0.66 us (1%)
    pallas_call x1, Pallas kernels, on_device(): pl.pallas_call(functools.partial(kernel, (n_level, n_band, channels, heig...  57.2 us
    unnamed x2, local copies, waits for them, and re-layouts  1.41 us
    concatenate x1, other arithmetic, on_device(): small = jnp.concatenate([eight(w_in), eight(w_out.T)], axis=0)  1.33 us

commit v1 on v0

--- a/solution.py
+++ b/solution.py
@@ -58,33 +58,43 @@
     return kept[0:1, 0:1]
 
 
-def pack_weights(raw, high_ref, low_ref, channels):
+def three_parts(v):
+    parts = []
+    for _ in range(3):
+        piece = v.astype(BF16).astype(F32)
+        parts.append(piece)
+        v = v - piece
+    return parts
+
+
+def pack_weights(n, raw, high_ref, low_ref, channels):
     rest = channels - 256
-    high_ref[:, 3 * channels :, :] = jnp.zeros((4, 1024 - 3 * channels, 256), BF16)
-    low_ref[:, 3 * channels :, :] = jnp.zeros((4, 1024 - 3 * channels, 256), BF16)
+    for ref in (high_ref, low_ref):
+        ref[n, 3 * channels :, :] = jnp.zeros((1024 - 3 * channels, 256), BF16)
     for b in range(3):
-        for n in range(4):
-            if n < 3:
-                piece = raw[n, b, :, 0:256]
-            else:
-                piece = jnp.concatenate(
-                    [raw[a, b, :, 256:channels] for a in range(3)]
-                    + [jnp.zeros((channels, 256 - 3 * rest), F32)],
-                    axis=1,
-                )
-            high, low = split(piece)
-            start = 768 + b * rest
-            high_ref[n, b * 256 : (b + 1) * 256, :] = high[0:256]
-            low_ref[n, b * 256 : (b + 1) * 256, :] = low[0:256]
-            high_ref[n, start : start + rest, :] = high[256:channels]
-            low_ref[n, start : start + rest, :] = low[256:channels]
+        if n < 3:
+            piece = raw[n, b, :, 0:256]
+        else:
+            piece = jnp.concatenate(
+                [raw[a, b, :, 256:channels] for a in range(3)]
+                + [jnp.zeros((channels, 256 - 3 * rest), F32)],
+                axis=1,
+            )
+        high, low = split(piece)
+        start = 768 + b * rest
+        high_ref[n, b * 256 : (b + 1) * 256, :] = high[0:256]
+        low_ref[n, b * 256 : (b + 1) * 256, :] = low[0:256]
+        high_ref[n, start : start + rest, :] = high[256:channels]
+        low_ref[n, start : start + rest, :] = low[256:channels]
 
 
 def kernel(
     sizes,
     step_ref,
-    pack_ref,
-    small_ref,
+    latents_ref,
+    fresh_ref,
+    w_in_ref,
+    w_out_ref,
     conv_first_hbm,
     conv_second_hbm,
     w_time_hbm,
@@ -103,6 +113,7 @@
     lifted_ref,
     value_ref,
     rest_ref,
+    pack_ref,
     gathered,
     send_frame,
     recv_frame,
@@ -135,9 +146,14 @@
             )
         )
     ]
-    for load in loads:
-        load.start()
-
+    loads[0].start()
+    loads[1].start()
+
+    lat = latents_ref.shape[1]
+    pack_ref[...] = jnp.zeros_like(pack_ref)
+    for r in range(latents_ref.shape[0]):
+        pack_ref[0:lat, r * width : (r + 1) * width] = latents_ref[r]
+        pack_ref[8 : 8 + lat, r * width : (r + 1) * width] = fresh_ref[r]
     recv_frame[...] = jnp.zeros_like(recv_frame)
     recv_tap[...] = jnp.zeros_like(recv_tap)
     recv_last[...] = jnp.zeros_like(recv_last)
@@ -176,8 +192,9 @@
     for i in range(n_band - 1):
         band_copy(i).start()
 
-    w_in = small_ref[0:8, :]
-    w_out = small_ref[8:16, :]
+    spare = jnp.zeros((8 - lat, channels), F32)
+    w_in = jnp.concatenate([w_in_ref[...], spare], axis=0)
+    w_out = jnp.concatenate([w_out_ref[...], spare], axis=0)
 
     per_group = channels // GROUPS
     def group_of(axis):
@@ -199,21 +216,15 @@
     harmonic = jnp.where(lane < half_width, jnp.cos(angle), jnp.sin(angle))
 
     loads[0].wait()
-    pack_weights(raw_first, first_high, first_low, channels)
+    loads[2].start()
+    loads[3].start()
+    for n in range(4):
+        pack_weights(n, raw_first, first_high, first_low, channels)
     loads[1].wait()
     embedded = silu(dot3(harmonic, raw_time[...]))[0:1, :]
-    loads[2].wait()
-    folded = jnp.concatenate(
-        [dot3(w_out, raw_temporal[k], NT) for k in range(3)]
-        + [jnp.zeros((8, channels), F32)],
-        axis=0,
-    )
-    folded_high, folded_low = split(folded)
     w_out_high, w_out_low = split(
         jnp.concatenate([w_out, jnp.zeros((24, channels), F32)], axis=0)
     )
-    loads[3].wait()
-    pack_weights(raw_second, second_high, second_low, channels)
 
     border = jnp.zeros((width, 1024), BF16)
     for ref in (act_high, act_low):
@@ -235,22 +246,46 @@
     frame = jnp.concatenate([p[0:8] for p in packs], axis=1)
     entering = jnp.concatenate([p[8:16] for p in packs], axis=1)
 
+    def over_chunks(body):
+        if height == chunk:
+            body(0)
+        else:
+            lax.fori_loop(0, height // chunk, lambda i, c: (body(i * chunk), c)[1], 0)
+
+    def image_row(i, count=1):
+        start = i * width
+        if not isinstance(start, int):
+            start = pl.multiple_of(start, width)
+        return pl.ds(start, count * width)
+
     def norm_terms(ref):
-        def add(i, sums):
-            part = ref[pl.ds(pl.multiple_of(i * block, block), block), :]
-            return (
-                sums[0] + jnp.sum(part, axis=0, keepdims=True),
-                sums[1] + jnp.sum(part * part, axis=0, keepdims=True),
-            )
-
-        zero = jnp.zeros((1, channels), F32)
-        sums = lax.fori_loop(0, height // chunk, add, (zero, zero))
+        def add(first):
+            sums = []
+            for i in range(chunk):
+                part = ref[image_row(first + i), :].reshape(width // 8, 8, channels)
+                sums.append((jnp.sum(part, axis=0), jnp.sum(part * part, axis=0)))
+            while len(sums) > 1:
+                pairs = [
+                    (x[0] + y[0], x[1] + y[1]) for x, y in zip(sums[0::2], sums[1::2])
+                ]
+                sums = pairs + sums[2 * len(pairs) :]
+            return sums[0]
+
+        if height == chunk:
+            sums = add(0)
+        else:
+            zero = jnp.zeros((8, channels), F32)
+
+            def more(i, carry):
+                part = add(i * chunk)
+                return carry[0] + part[0], carry[1] + part[1]
+
+            sums = lax.fori_loop(0, height // chunk, more, (zero, zero))
         row = lax.broadcasted_iota(jnp.int32, (16, channels), 0)
         stacked = jnp.zeros((16, channels), F32)
         for which, left in enumerate(sums):
-            for part in range(3):
-                piece = left.astype(BF16).astype(F32)
-                left = left - piece
+            left = jnp.sum(left, axis=0, keepdims=True)
+            for part, piece in enumerate(three_parts(left)):
                 stacked = jnp.where(row == which * 3 + part, piece, stacked)
         totals = dot(stacked.astype(BF16), same_group)
         members = float(pixels * per_group)
@@ -263,58 +298,63 @@
     def fill_act(ref, terms):
         center, factor = terms
 
-        def one_row(i, carry):
-            v = silu((ref[pl.ds(pl.multiple_of(i * width, width), width), :] - center) * factor)
-            before = jnp.where(column == 0, 0.0, pltpu.roll(v, 1, 0))
-            after = jnp.where(column == width - 1, 0.0, pltpu.roll(v, width - 1, 0))
-            taps = (before, v, after)
-            wide = jnp.concatenate(
-                [t[:, 0:256] for t in taps]
-                + [t[:, 256:channels] for t in taps]
-                + [jnp.zeros((width, 1024 - 3 * channels), F32)],
-                axis=1,
+        def rows(first):
+            for i in range(chunk):
+                v = silu((ref[image_row(first + i), :] - center) * factor)
+                before = jnp.where(column == 0, 0.0, pltpu.roll(v, 1, 0))
+                after = jnp.where(column == width - 1, 0.0, pltpu.roll(v, width - 1, 0))
+                taps = (before, v, after)
+                wide = jnp.concatenate(
+                    [t[:, 0:256] for t in taps]
+                    + [t[:, 256:channels] for t in taps]
+                    + [jnp.zeros((width, 1024 - 3 * channels), F32)],
+                    axis=1,
+                )
+                high, low = split(wide)
+                act_high[image_row(first + i + 1), :] = high
+                act_low[image_row(first + i + 1), :] = low
+
+        over_chunks(rows)
+
+    half = chunk // 2 if chunk % 2 == 0 else chunk
+
+    def convolve(high_ref, low_ref, add, beside=None):
+        def depth(first, n):
+            left = act_high[image_row(first, half), :]
+            return (
+                [left, act_low[image_row(first, half), :], left],
+                [high_ref[n], high_ref[n], low_ref[n]],
             )
-            high, low = split(wide)
-            place = pl.ds(pl.multiple_of((i + 1) * width, width), width)
-            act_high[place, :] = high
-            act_low[place, :] = low
-            return carry
-
-        lax.fori_loop(0, height, one_row, 0)
-
-    def convolve(high_ref, low_ref, add):
-        def product(start, n):
-            place = pl.ds(pl.multiple_of(start, width), block)
-            left = act_high[place, :]
-            return (
-                dot(left, high_ref[n])
-                + dot(act_low[place, :], high_ref[n])
-                + dot(left, low_ref[n])
+
+        def product(*terms):
+            return dot(
+                jnp.concatenate([x for left, _ in terms for x in left], axis=1),
+                jnp.concatenate([x for _, right in terms for x in right], axis=0),
             )
 
-        def part(i, carry):
-            base = i * block
-            rest_ref[pl.ds(pl.multiple_of(base + width, width), block), :] = product(
-                base + width, 3
-            )
-            total = product(base, 0) + product(base + width, 1)
-            total = total + product(base + 2 * width, 2)
-            place = pl.ds(pl.multiple_of(base, width), block)
-            value_ref[place, 0:256] = total + add(place)[:, 0:256]
-            return carry
-
-        lax.fori_loop(0, height // chunk, part, 0)
-
-        def end(i, carry):
-            base = i * width
-            total = add(pl.ds(pl.multiple_of(base, width), width))[:, 256:channels]
-            for a in range(3):
-                rows = pl.ds(pl.multiple_of(base + a * width, width), width)
-                total = total + rest_ref[rows, a * rest : (a + 1) * rest]
-            value_ref[pl.ds(pl.multiple_of(base, width), width), 256:channels] = total
-            return carry
-
-        lax.fori_loop(0, height, end, 0)
+        def rows(first):
+            for i in range(0, chunk, half):
+                at = first + i
+                rest_ref[image_row(at + 1, half), :] = product(depth(at + 1, 3))
+            for i in range(0, chunk, half):
+                at = first + i
+                total = product(depth(at, 0), depth(at + 1, 1), depth(at + 2, 2))
+                place = image_row(at, half)
+                value_ref[place, 0:256] = total + add(place)[:, 0:256]
+
+        over_chunks(rows)
+        if beside is not None:
+            beside()
+
+        def end(first):
+            for i in range(chunk):
+                place = image_row(first + i)
+                total = add(place)[:, 256:channels]
+                for a in range(3):
+                    total = total + rest_ref[image_row(first + i + a), a * rest : (a + 1) * rest]
+                value_ref[place, 256:channels] = total
+
+        over_chunks(end)
 
     def project(high, low, values):
         vh, vl = split(values)
@@ -331,21 +371,36 @@
             device_id_type=MESH,
         )
 
-    def run_block(frame):
-        lifted_ref[...] = lax.dot_general(
-            frame.T, w_in, NN, precision=lax.Precision.HIGHEST, preferred_element_type=F32
-        )
+    wh, wm, wl = three_parts(w_in)
+    w_in_parts = jnp.concatenate([wh, wm, wh, wm, wl, wh], axis=0).astype(BF16)
+
+    def run_block(frame, beside=None):
+        xh, xm, xl = three_parts(frame)
+        left = jnp.concatenate([xh, xh, xm, xm, xh, xl], axis=0).T.astype(BF16)
+        lifted_ref[...] = dot(left, w_in_parts)
         fill_act(lifted_ref, norm_terms(lifted_ref))
-        convolve(first_high, first_low, lambda place: embedded)
+        convolve(first_high, first_low, lambda place: embedded, beside)
         fill_act(value_ref, norm_terms(value_ref))
         convolve(second_high, second_low, lambda place: lifted_ref[place, :])
-        return norm_terms(value_ref)
-
-    center, factor = run_block(frame)
+
+    def prepare_later():
+        for n in range(4):
+            pack_weights(n, raw_second, second_high, second_low, channels)
+
+    loads[2].wait()
+    loads[3].wait()
+    folded = jnp.concatenate(
+        [dot3(w_out, raw_temporal[k], NT) for k in range(3)]
+        + [jnp.zeros((8, channels), F32)],
+        axis=0,
+    )
+    folded_high, folded_low = split(folded)
+    run_block(frame, prepare_later)
     hidden = value_ref[...]
+    straight = project(w_out_high, w_out_low, hidden)[0:8]
+    center, factor = norm_terms(value_ref)
     taps = project(folded_high, folded_low, silu((hidden - center) * factor))
-    local = project(w_out_high, w_out_low, hidden)[0:8] + taps[8:16]
-    send_frame[0:8, :] = scale_x * frame + scale_noise * local
+    send_frame[0:8, :] = scale_x * frame + scale_noise * (straight + taps[8:16])
     send_frame[8:16, :] = jnp.broadcast_to(scale_noise, (8, pixels))
     send_tap[...] = taps[0:8]
     frame_copy = level_copy(0, send_frame, recv_frame, level + 1)
@@ -359,8 +414,10 @@
     pl.when(has_two_up)(lambda: tap_copy.wait_send())
     pl.when(has_up)(lambda: frame_copy.wait_send())
 
-    center, factor = run_block(frame)
+    run_block(frame)
     hidden = value_ref[pl.ds(pl.multiple_of(band * held, width), held), :]
+    straight = project(w_out_high, w_out_low, hidden)[0:8]
+    center, factor = norm_terms(value_ref)
     taps = project(folded_high, folded_low, silu((hidden - center) * factor))
     send_last[0] = taps[0:8]
     send_last[1] = taps[16:24]
@@ -368,13 +425,15 @@
     down_copy = level_copy(3, send_last.at[1], recv_last.at[1], level - 1)
     pl.when(has_up)(lambda: up_copy.start())
     pl.when(has_down)(lambda: down_copy.start())
-    local = project(w_out_high, w_out_low, hidden)[0:8] + taps[8:16]
+    local = straight + taps[8:16]
     mine = frame[:, 0:held]
     for j in range(1, n_band):
         mine = jnp.where(band == j, frame[:, j * held : (j + 1) * held], mine)
     pl.when(has_down)(lambda: up_copy.wait_recv())
     pl.when(has_up)(lambda: down_copy.wait_recv())
-    out_ref[...] = scale_x * mine + scale_noise * (local + recv_last[0] + recv_last[1])
+    done = scale_x * mine + scale_noise * (local + recv_last[0] + recv_last[1])
+    for r in range(out_ref.shape[0]):
+        out_ref[r] = done[0:lat, r * width : (r + 1) * width]
     pl.when(has_up)(lambda: up_copy.wait_send())
     pl.when(has_down)(lambda: down_copy.wait_send())
 
@@ -390,21 +449,13 @@
     held = band_rows * width
     chunk = max(d for d in range(1, 11) if height % d == 0)
 
-    def eight(rows):
-        return jnp.pad(rows, ((0, 8 - lat), (0, 0)))
-
-    pack = jnp.concatenate(
-        [eight(latents[0].reshape(lat, held)), eight(fresh[0].reshape(lat, held))], axis=0
-    )
-    small = jnp.concatenate([eight(w_in), eight(w_out.T)], axis=0)
-
     vmem = pl.BlockSpec(memory_space=pltpu.VMEM)
     hbm = pl.BlockSpec(memory_space=pl.ANY)
     sem = pltpu.SemaphoreType.DMA
     result = pl.pallas_call(
         functools.partial(kernel, (n_level, n_band, channels, height, width, chunk)),
-        out_shape=jax.ShapeDtypeStruct((8, held), F32),
-        in_specs=[pl.BlockSpec(memory_space=pltpu.SMEM), vmem, vmem, hbm, hbm, hbm, hbm],
+        out_shape=jax.ShapeDtypeStruct((band_rows, lat, width), F32),
+        in_specs=[pl.BlockSpec(memory_space=pltpu.SMEM)] + [vmem] * 4 + [hbm] * 4,
         out_specs=vmem,
         scratch_shapes=[
             pltpu.VMEM(conv_first.shape, F32),
@@ -415,6 +466,7 @@
             *[pltpu.VMEM((pixels + 2 * width, 1024), BF16)] * 2,
             *[pltpu.VMEM((pixels, channels), F32)] * 2,
             pltpu.VMEM((pixels + 2 * width, 256), F32),
+            pltpu.VMEM((16, held), F32),
             pltpu.VMEM((max(n_band - 1, 1), 16, held), F32),
             *[pltpu.VMEM((16, pixels), F32)] * 2,
             *[pltpu.VMEM((8, pixels), F32)] * 2,
@@ -428,8 +480,18 @@
         compiler_params=pltpu.CompilerParams(
             collective_id=0, has_side_effects=True, vmem_limit_bytes=60 * 1024 * 1024
         ),
-    )(timesteps, pack, small, conv_first, conv_second, w_time, temporal)
-    return result[0:lat].reshape(1, lat, band_rows, width)
+    )(
+        timesteps,
+        latents[0].transpose(1, 0, 2),
+        fresh[0].transpose(1, 0, 2),
+        w_in,
+        w_out.T,
+        conv_first,
+        conv_second,
+        w_time,
+        temporal,
+    )
+    return result.transpose(1, 0, 2)[None]
 
 
 def solution(mesh):

time: 62.6 us -> 38.5 us (0.62)
  Pallas kernels: 57.2 us -> 36.2 us
  local copies, waits for them, and re-layouts: 2.96 us -> 1.3 us
  other arithmetic: 1.33 us -> 0 us
    pallas_call x1, Pallas kernels: 57.2 us -> 36.2 us  [on_device(): pl.pallas_call(functools.partial(kernel, (n_level, n_band, channels, heig...]
    concatenate x1 -> x0, other arithmetic: 1.33 us -> none  [on_device(): small = jnp.concatenate([eight(w_in), eight(w_out.T)], axis=0)]
    slice x1 -> x0, local copies, waits for them, and re-layouts: 0.71 us -> none  [on_device(): return result[0:lat].reshape(1, lat, band_rows, width)]
    reshape x2 -> x0, local copies, waits for them, and re-layouts: 0.68 us -> none  [on_device(): return result[0:lat].reshape(1, lat, band_rows, width)]
    unnamed x2 -> x1, local copies, waits for them, and re-layouts: 1.41 us -> 1.3 us
where the time goes in v1:
time: 38.5 us; the launch traced here: 38.2 us
  Pallas kernels  36.2 us (94%)
  local copies, waits for them, and re-layouts  1.3 us (3%)
  between operations  0.66 us (2%)
    pallas_call x1, Pallas kernels, on_device(): pl.pallas_call(functools.partial(kernel, (n_level, n_band, channels, heig...  36.2 us
    unnamed x1, local copies, waits for them, and re-layouts  1.3 us

profile of v1, /device:TPU:23, one launch (start us, length us, event | category | flops | bytes accessed | tf_op | source)
XLA Modules:
  0.0 38.2 jit_solution(5190091134138037365)
XLA Ops:
  0.7 36.2 %shard_map.91 = f32[5,4,64]{2,1,0:T(4,128)} custom-call(s32[1]{0:T(128)S(6)} %copy.11.step_ref, f32[5,4,64]{2,1,0:T(4,128)} %bitcast.11, f32[5,4,64]{2,1,0:T(4,128)} %bitcast.12, f32[4,320]{1,0:T(4,128)} %w_in_ref.1, f32[4,320]{1,0:T(4,128)} %bitcast.13, f32[3,3,320,320]{3,2,1,0:T(8,128)} %conv_first_hbm.1, f32[3,3,320,320]{3,2,1,0:T(8,128)} %conv_second_hbm.1, ...), custom_call_target="tpu_custom_call" | custom-call | tf_op jit(solution)/shard_map/pallas_call | solution.py:455
  36.9 1.3 %copy.12 = f32[1,4,5,64]{3,1,2,0:T(4,128)} copy(f32[1,4,5,64]{3,1,2,0:T(4,128)} %bitcast.10) | data formatting | bytes 10240

commit v2 on v1

v2 whole, which is shorter than its diff:
```python
import functools
import math

import jax
import jax.numpy as jnp
from jax import lax
from jax.experimental import pallas as pl
from jax.experimental.pallas import tpu as pltpu
from jax.sharding import PartitionSpec as P

GROUPS = 32
ITERS = 2
NSTEPS = 1000
STRIDE = 16
EPSILON = 1e-05

MESH = pl.DeviceIdType.MESH
F32 = jnp.float32
BF16 = jnp.bfloat16
NN = (((1,), (0,)), ((), ()))
NT = (((1,), (1,)), ((), ()))
TN = (((0,), (0,)), ((), ()))


def dot(a, b, dims=NN):
    return lax.dot_general(a, b, dims, preferred_element_type=F32)


def split(v):
    high = v.astype(BF16)
    return high, (v - high.astype(F32)).astype(BF16)


def dot3(a, b, dims=NN):
    ah, al = split(a)
    bh, bl = split(b)
    return dot(ah, bh, dims) + dot(al, bh, dims) + dot(ah, bl, dims)


def silu(v):
    half = 0.5 * v
    return half + half * jnp.tanh(half)


def plan_at(step):
    rows = -(-NSTEPS // 1024) * 8
    position = lax.broadcasted_iota(jnp.int32, (rows, 128), 0) * 128
    position = position + lax.broadcasted_iota(jnp.int32, (rows, 128), 1)
    root_beta = math.sqrt(0.00085) + position.astype(F32) / (NSTEPS - 1) * (
        math.sqrt(0.012) - math.sqrt(0.00085)
    )
    kept = jnp.where(position <= step, 1.0 - root_beta * root_beta, 1.0)
    for axis, length in ((0, rows), (1, 128)):
        shift = length // 2
        while shift:
            kept = kept * pltpu.roll(kept, shift, axis)
            shift //= 2
    return kept[0:1, 0:1]


def three_parts(v):
    parts = []
    for _ in range(3):
        piece = v.astype(BF16).astype(F32)
        parts.append(piece)
        v = v - piece
    return parts


def pack_weights(n, raw, high_ref, low_ref, channels):
    rest = channels - 256
    for ref in (high_ref, low_ref):
        ref[n, 3 * channels :, :] = jnp.zeros((1024 - 3 * channels, 256), BF16)
    for b in range(3):
        if n < 3:
            piece = raw[n, b, :, 0:256]
        else:
            piece = jnp.concatenate(
                [raw[a, b, :, 256:channels] for a in range(3)]
                + [jnp.zeros((channels, 256 - 3 * rest), F32)],
                axis=1,
            )
        high, low = split(piece)
        start = 768 + b * rest
        high_ref[n, b * 256 : (b + 1) * 256, :] = high[0:256]
        low_ref[n, b * 256 : (b + 1) * 256, :] = low[0:256]
        high_ref[n, start : start + rest, :] = high[256:channels]
        low_ref[n, start : start + rest, :] = low[256:channels]


def kernel(
    sizes,
    step_hbm,
    latents_hbm,
    fresh_hbm,
    w_in_hbm,
    w_out_hbm,
    conv_first_hbm,
    conv_second_hbm,
    w_time_hbm,
    temporal_hbm,
    out_ref,
    step_ref,
    latents_ref,
    fresh_ref,
    w_in_ref,
    w_out_ref,
    raw_first,
    raw_second,
    raw_time,
    raw_temporal,
    first_high,
    first_low,
    second_high,
    second_low,
    act_high,
    act_low,
    lifted_ref,
    first_ref,
    hidden_ref,
    rest_ref,
    pack_ref,
    gathered,
    stat_mine,
    stat_theirs,
    send_frame,
    recv_frame,
    send_tap,
    recv_tap,
    send_back,
    recv_back,
    send_last,
    recv_last,
    load_sem,
    band_send,
    band_recv,
    stat_send,
    stat_recv,
    frame_send,
    frame_recv,
    tap_send,
    tap_recv,
    back_send,
    back_recv,
    last_send,
    last_recv,
):
    n_level, n_band, channels, height, width, n_first = sizes
    rest = channels - 256
    pixels = height * width
    own = height // n_band
    held = own * width
    level = lax.axis_index("level")
    band = lax.axis_index("band")
    start = jnp.where(band == n_band - 1, height - n_first, band * own - 1)
    start = jnp.where(band == 0, 0, start)
    inset = band * own - start

    loads = [
        pltpu.make_async_copy(source, target, load_sem.at[i])
        for i, (source, target) in enumerate(
            (
                (latents_hbm, latents_ref),
                (fresh_hbm, fresh_ref),
                (step_hbm, step_ref),
                (w_in_hbm, w_in_ref),
                (w_out_hbm, w_out_ref),
                (conv_first_hbm, raw_first),
                (w_time_hbm, raw_time),
                (temporal_hbm, raw_temporal),
                (conv_second_hbm, raw_second),
            )
        )
    ]
    for load in loads[:7]:
        load.start()

    recv_frame[...] = jnp.zeros_like(recv_frame)
    recv_tap[...] = jnp.zeros_like(recv_tap)
    recv_last[...] = jnp.zeros_like(recv_last)

    has_up = level + 1 < n_level
    has_two_up = level + 2 < n_level
    has_down = level >= 1
    has_two_down = level >= 2

    barrier = pltpu.get_barrier_semaphore()
    others = [lax.rem(band + i, n_band) for i in range(n_band)]
    peers = others[1:]

    def greet(*who):
        for one in who:
            pl.semaphore_signal(barrier, inc=1, device_id=one, device_id_type=MESH)

    greet(*[{"band": peer} for peer in peers])
    pl.when(has_down)(lambda: greet(*[{"level": level - 1, "band": o} for o in others]))
    pl.when(has_two_down)(lambda: greet(*[{"level": level - 2, "band": o} for o in others]))
    pl.when(has_up)(lambda: greet({"level": level + 1}))

    lat = latents_ref.shape[1]
    pack_ref[...] = jnp.zeros_like(pack_ref)
    loads[0].wait()
    loads[1].wait()
    for r in range(own):
        pack_ref[0:lat, r * width : (r + 1) * width] = latents_ref[r]
        pack_ref[8 : 8 + lat, r * width : (r + 1) * width] = fresh_ref[r]

    expected = n_band - 1
    for there, count in ((has_up, n_band), (has_two_up, n_band), (has_down, 1)):
        expected = expected + jnp.where(there, count, 0)
    pl.semaphore_wait(barrier, expected)

    def remote(source, target, sent, arrived, to):
        return pltpu.make_async_remote_copy(
            src_ref=source,
            dst_ref=target,
            send_sem=sent,
            recv_sem=arrived,
            device_id=to,
            device_id_type=MESH,
        )

    band_copies = [
        remote(pack_ref, gathered.at[i], band_send.at[i], band_recv.at[i], {"band": peers[i]})
        for i in range(n_band - 1)
    ]
    for copy in band_copies:
        copy.start()

    def by_band(slots):
        found = []
        for j in range(n_band):
            block = slots[0]
            for i in range(1, n_band):
                block = jnp.where(lax.rem(band - i + n_band, n_band) == j, slots[i], block)
            found.append(block)
        return found

    per_group = channels // GROUPS

    def group_of(axis):
        index = lax.broadcasted_iota(jnp.int32, (channels, channels), axis).astype(F32)
        return jnp.floor((index + 0.5) * (1.0 / per_group))

    same_group = jnp.where(group_of(0) == group_of(1), 1.0, 0.0).astype(BF16)

    for load in loads[2:5]:
        load.wait()
    spare = jnp.zeros((8 - lat, channels), F32)
    w_in = jnp.concatenate([w_in_ref[...], spare], axis=0)
    w_out = jnp.concatenate([w_out_ref[...], spare], axis=0)
    wh, wm, wl = three_parts(w_in)
    w_in_parts = jnp.concatenate([wh, wm, wh, wm, wl, wh], axis=0).astype(BF16)

    step = step_ref[0]
    alpha_now = plan_at(step)
    alpha_prev = plan_at(step - STRIDE)
    scale_x = jnp.sqrt(alpha_prev) / jnp.sqrt(alpha_now)
    scale_noise = jnp.sqrt(1.0 - alpha_prev) - scale_x * jnp.sqrt(1.0 - alpha_now)

    lane = lax.broadcasted_iota(jnp.int32, (8, channels), 1)
    half_width = channels // 2
    harmonic_index = jnp.where(lane < half_width, lane, lane - half_width).astype(F32)
    frequency = jnp.exp(-math.log(10000.0) * harmonic_index / half_width)
    angle = step.astype(F32) * frequency
    harmonic = jnp.where(lane < half_width, jnp.cos(angle), jnp.sin(angle))

    lifted_ref[0:width, :] = jnp.zeros((width, channels), F32)
    lifted_ref[width + pixels :, :] = jnp.zeros((width, channels), F32)
    first_ref[0:width, :] = jnp.zeros((width, channels), F32)
    first_ref[(n_first + 1) * width :, :] = jnp.zeros((width, channels), F32)
    rest_ref[...] = jnp.zeros_like(rest_ref)

    loads[5].wait()
    loads[7].start()
    loads[8].start()
    for n in range(4):
        pack_weights(n, raw_first, first_high, first_low, channels)
    loads[6].wait()
    embedded = silu(dot3(harmonic, raw_time[...]))[0:1, :]
    w_out_high, w_out_low = split(
        jnp.concatenate([w_out, jnp.zeros((24, channels), F32)], axis=0)
    )

    for copy in band_copies:
        copy.wait()

    packs = by_band([pack_ref[...]] + [gathered[i] for i in range(n_band - 1)])
    frame = jnp.concatenate([p[0:8] for p in packs], axis=1)
    entering = jnp.concatenate([p[8:16] for p in packs], axis=1)

    def image_row(i, count=1):
        at = i * width
        if not isinstance(at, int):
            at = pl.multiple_of(at, width)
        return pl.ds(at, count * width)

    def local_sums(ref, first, count):
        sums = []
        for i in range(count):
            part = ref[image_row(first + i), :].reshape(width // 8, 8, channels)
            sums.append((jnp.sum(part, axis=0), jnp.sum(part * part, axis=0)))
        while len(sums) > 1:
            pairs = [(x[0] + y[0], x[1] + y[1]) for x, y in zip(sums[0::2], sums[1::2])]
            sums = pairs + sums[2 * len(pairs) :]
        return [jnp.sum(x, axis=0, keepdims=True) for x in sums[0]]

    def norm_terms(sums):
        row = lax.broadcasted_iota(jnp.int32, (16, channels), 0)
        stacked = jnp.zeros((16, channels), F32)
        for which, left in enumerate(sums):
            for part, piece in enumerate(three_parts(left)):
                stacked = jnp.where(row == which * 3 + part, piece, stacked)
        totals = dot(stacked.astype(BF16), same_group)
        members = float(pixels * per_group)
        center = (totals[0:1] + totals[1:2] + totals[2:3]) / members
        square = (totals[3:4] + totals[4:5] + totals[5:6]) / members
        return center, lax.rsqrt(square - center * center + EPSILON)

    def shared_terms(turn, ref, first):
        sums = local_sums(ref, first, own)
        stat_mine[turn, 0:1, :] = sums[0]
        stat_mine[turn, 1:2, :] = sums[1]
        stat_mine[turn, 2:8, :] = jnp.zeros((6, channels), F32)
        copies = [
            remote(
                stat_mine.at[turn],
                stat_theirs.at[turn, i],
                stat_send.at[turn, i],
                stat_recv.at[turn, i],
                {"band": peers[i]},
            )
            for i in range(n_band - 1)
        ]
        for copy in copies:
            copy.start()
        for copy in copies:
            copy.wait()
        for i in range(n_band - 1):
            sums = [x + stat_theirs[turn, i, w : w + 1, :] for w, x in enumerate(sums)]
        return norm_terms(sums)

    column = lax.broadcasted_iota(jnp.int32, (width, channels), 0)

    def fill_act(ref, first, top, count, terms):
        center, factor = terms
        for i in range(count):
            v = silu((ref[image_row(first + i), :] - center) * factor)
            if i == 0:
                v = jnp.where(top < 0, 0.0, v)
            if i == count - 1:
                v = jnp.where(top + i >= height, 0.0, v)
            before = jnp.where(column == 0, 0.0, pltpu.roll(v, 1, 0))
            after = jnp.where(column == width - 1, 0.0, pltpu.roll(v, width - 1, 0))
            taps = (before, v, after)
            wide = jnp.concatenate(
                [t[:, 0:256] for t in taps]
                + [t[:, 256:channels] for t in taps]
                + [jnp.zeros((width, 1024 - 3 * channels), F32)],
                axis=1,
            )
            high, low = split(wide)
            act_high[image_row(i), :] = high
            act_low[image_row(i), :] = low

    def convolve(high_ref, low_ref, count, add, out, out_first, beside=None):
        part = max(d for d in range(1, 7) if count % d == 0)

        def depth(first, n, size):
            left = act_high[image_row(first, size), :]
            return (
                [left, act_low[image_row(first, size), :], left],
                [high_ref[n], high_ref[n], low_ref[n]],
            )

        def product(*terms):
            return dot(
                jnp.concatenate([x for left, _ in terms for x in left], axis=1),
                jnp.concatenate([x for _, right in terms for x in right], axis=0),
            )

        filled = count + 2
        share = max(d for d in range(1, 8) if filled % d == 0)
        for i in range(0, filled, share):
            rest_ref[image_row(i, share), :] = product(depth(i, 3, share))
        for i in range(0, count, part):
            total = product(depth(i, 0, part), depth(i + 1, 1, part), depth(i + 2, 2, part))
            out[image_row(out_first + i, part), 0:256] = total + add(i, part)[:, 0:256]
        if beside is not None:
            beside()
        for i in range(count):
            total = add(i, 1)[:, 256:channels]
            for a in range(3):
                total = total + rest_ref[image_row(i + a), a * rest : (a + 1) * rest]
            out[image_row(out_first + i), 256:channels] = total

    def project(high, low, values):
        vh, vl = split(values)
        both = dot(jnp.concatenate([high, low], axis=0), vh, NT)
        return both[0:32] + both[32:64] + dot(high, vl, NT)

    def run_block(iteration, frame, beside=None):
        xh, xm, xl = three_parts(frame)
        left = jnp.concatenate([xh, xh, xm, xm, xh, xl], axis=0).T.astype(BF16)
        lifted_ref[width : width + pixels, :] = dot(left, w_in_parts)
        terms = norm_terms(local_sums(lifted_ref, 1, height))
        fill_act(lifted_ref, start, start - 1, n_first + 2, terms)
        convolve(
            first_high, first_low, n_first, lambda i, size: embedded, first_ref, 1, beside
        )
        terms = shared_terms(2 * iteration, first_ref, 1 + inset)
        fill_act(first_ref, inset, band * own - 1, own + 2, terms)
        convolve(
            second_high,
            second_low,
            own,
            lambda i, size: lifted_ref[image_row(band * own + 1 + i, size), :],
            hidden_ref,
            0,
        )
        hidden = hidden_ref[...]
        straight = project(w_out_high, w_out_low, hidden)[0:8]
        center, factor = shared_terms(2 * iteration + 1, hidden_ref, 0)
        taps = project(folded_high, folded_low, silu((hidden - center) * factor))
        return straight + taps[8:16], taps

    def mine_of(frame):
        mine = frame[:, 0:held]
        for j in range(1, n_band):
            mine = jnp.where(band == j, frame[:, j * held : (j + 1) * held], mine)
        return mine

    def prepare_later():
        for n in range(4):
            pack_weights(n, raw_second, second_high, second_low, channels)

    loads[7].wait()
    loads[8].wait()
    folded = jnp.concatenate(
        [dot3(w_out, raw_temporal[k], NT) for k in range(3)]
        + [jnp.zeros((8, channels), F32)],
        axis=0,
    )
    folded_high, folded_low = split(folded)

    local, taps = run_block(0, frame, prepare_later)
    send_tap[...] = taps[0:8]
    send_back[...] = taps[16:24]
    tap_copies = [
        remote(
            send_tap, recv_tap.at[i], tap_send.at[i], tap_recv.at[i], {"level": level + 2, "band": o}
        )
        for i, o in enumerate(others)
    ]
    frame_copies = [
        remote(
            send_frame,
            recv_frame.at[i],
            frame_send.at[i],
            frame_recv.at[i],
            {"level": level + 1, "band": o},
        )
        for i, o in enumerate(others)
    ]
    back_copies = [
        remote(send_back, recv_back.at[i], back_send.at[i], back_recv.at[i], {"band": peers[i]})
        for i in range(n_band - 1)
    ]

    def each(action, copies):
        for copy in copies:
            getattr(copy, action)()

    pl.when(has_two_up)(lambda: each("start", tap_copies))
    send_frame[0:4, :] = (scale_x * mine_of(frame) + scale_noise * local)[0:4]
    send_frame[4:8, :] = jnp.broadcast_to(scale_noise, (4, held))
    pl.when(has_up)(lambda: each("start", frame_copies))
    each("start", back_copies)
    each("wait", back_copies)
    pl.when(has_two_down)(lambda: each("wait_recv", tap_copies))
    pl.when(has_down)(lambda: each("wait_recv", frame_copies))
    slots = [taps[16:24]] + [recv_back[i] for i in range(n_band - 1)]
    moved = []
    for i in range(n_band):
        turned = recv_frame[i][4:8] * (recv_tap[i] + slots[i])[0:4]
        moved.append(recv_frame[i][0:4] + turned)
    moved = jnp.concatenate(by_band(moved), axis=1)
    moved = jnp.concatenate([moved, jnp.zeros((4, pixels), F32)], axis=0)
    frame = jnp.where(level == 0, entering, moved)
    pl.when(has_two_up)(lambda: each("wait_send", tap_copies))
    pl.when(has_up)(lambda: each("wait_send", frame_copies))

    local, taps = run_block(1, frame)
    send_last[0] = taps[0:8]
    send_last[1] = taps[16:24]
    up_copy, down_copy = (
        remote(
            send_last.at[i], recv_last.at[i], last_send.at[i], last_recv.at[i], {"level": to}
        )
        for i, to in enumerate((level + 1, level - 1))
    )
    pl.when(has_up)(lambda: up_copy.start())
    pl.when(has_down)(lambda: down_copy.start())
    done = scale_x * mine_of(frame) + scale_noise * local
    pl.when(has_down)(lambda: up_copy.wait_recv())
    pl.when(has_up)(lambda: down_copy.wait_recv())
    done = done + scale_noise * (recv_last[0] + recv_last[1])
    for r in range(own):
        out_ref[r] = done[0:lat, r * width : (r + 1) * width]
    pl.when(has_up)(lambda: up_copy.wait_send())
    pl.when(has_down)(lambda: down_copy.wait_send())


def on_device(
    mesh_sizes, latents, timesteps, fresh, w_in, conv_first, conv_second, w_time, temporal, w_out
):
    n_level, n_band = mesh_sizes
    lat, band_rows, width = latents.shape[1:]
    channels = w_in.shape[1]
    height = band_rows * n_band
    pixels = height * width
    held = band_rows * width
    n_first = min(height, band_rows + min(n_band - 1, 2))
    others = max(n_band - 1, 1)

    vmem = pl.BlockSpec(memory_space=pltpu.VMEM)
    hbm = pl.BlockSpec(memory_space=pl.ANY)
    sem = pltpu.SemaphoreType.DMA
    result = pl.pallas_call(
        functools.partial(kernel, (n_level, n_band, channels, height, width, n_first)),
        out_shape=jax.ShapeDtypeStruct((band_rows, lat, width), F32),
        in_specs=[hbm] * 9,
        out_specs=vmem,
        scratch_shapes=[
            pltpu.SMEM((1,), jnp.int32),
            *[pltpu.VMEM((band_rows, lat, width), F32)] * 2,
            *[pltpu.VMEM((lat, channels), F32)] * 2,
            pltpu.VMEM(conv_first.shape, F32),
            pltpu.VMEM(conv_second.shape, F32),
            pltpu.VMEM(w_time.shape, F32),
            pltpu.VMEM(temporal.shape, F32),
            *[pltpu.VMEM((4, 1024, 256), BF16)] * 4,
            *[pltpu.VMEM(((n_first + 2) * width, 1024), BF16)] * 2,
            pltpu.VMEM(((height + 2) * width, channels), F32),
            pltpu.VMEM(((n_first + 2) * width, channels), F32),
            pltpu.VMEM((held, channels), F32),
            pltpu.VMEM(((n_first + 2) * width, 256), F32),
            pltpu.VMEM((16, held), F32),
            pltpu.VMEM((others, 16, held), F32),
            pltpu.VMEM((2 * ITERS, 8, channels), F32),
            pltpu.VMEM((2 * ITERS, others, 8, channels), F32),
            *[pltpu.VMEM((8, held), F32), pltpu.VMEM((n_band, 8, held), F32)] * 2,
            *[pltpu.VMEM((8, held), F32), pltpu.VMEM((others, 8, held), F32)],
            *[pltpu.VMEM((2, 8, held), F32)] * 2,
            sem((9,)),
            *[sem((others,))] * 2,
            *[sem((2 * ITERS, others))] * 2,
            *[sem((n_band,))] * 4,
            *[sem((others,))] * 2,
            *[sem((2,))] * 2,
        ],
        compiler_params=pltpu.CompilerParams(
            collective_id=0, has_side_effects=True, vmem_limit_bytes=60 * 1024 * 1024
        ),
    )(
        timesteps,
        latents[0].transpose(1, 0, 2),
        fresh[0].transpose(1, 0, 2),
        w_in,
        w_out.T,
        conv_first,
        conv_second,
        w_time,
        temporal,
    )
    return result.transpose(1, 0, 2)[None]


def solution(mesh):
    placed = (
        P("level", None, "band", None),
        P("level"),
        P(None, None, "band", None),
        P(),
        P(),
        P(),
        P(),
        P(),
        P(),
    )
    return jax.shard_map(
        functools.partial(on_device, (mesh.shape["level"], mesh.shape["band"])),
        mesh=mesh,
        in_specs=placed,
        out_specs=P("level", None, "band", None),
        check_vma=False,
    )
```

time: 38.5 us -> 50.8 us (1.32)
  Pallas kernels: 36.2 us -> 48.3 us
    pallas_call x1, Pallas kernels: 36.2 us -> 48.3 us  [on_device(): pl.pallas_call(functools.partial(kernel, (n_level, n_band, channels, heig...]
where the time goes in v2:
time: 50.8 us; the launch traced here: 50.2 us
  Pallas kernels  48.3 us (95%)
  local copies, waits for them, and re-layouts  1.3 us (3%)
  between operations  0.66 us (1%)
    pallas_call x1, Pallas kernels, on_device(): pl.pallas_call(functools.partial(kernel, (n_level, n_band, channels, heig...  48.3 us
    unnamed x1, local copies, waits for them, and re-layouts  1.3 us

profile of v2, /device:TPU:23, one launch (start us, length us, event | category | flops | bytes accessed | tf_op | source)
XLA Modules:
  0.0 50.2 jit_solution(18076930188839873933)
XLA Ops:
  0.7 48.3 %shard_map.91 = f32[5,4,64]{2,1,0:T(4,128)} custom-call(s32[1]{0:T(128)S(6)} %copy.11.step_hbm, f32[5,4,64]{2,1,0:T(4,128)} %bitcast.11, f32[5,4,64]{2,1,0:T(4,128)} %bitcast.12, f32[4,320]{1,0:T(4,128)} %w_in_hbm.1, f32[4,320]{1,0:T(4,128)} %bitcast.13, f32[3,3,320,320]{3,2,1,0:T(8,128)} %conv_first_hbm.1, f32[3,3,320,320]{3,2,1,0:T(8,128)} %conv_second_hbm.1, ...), custom_call_target="tpu_custom_call" | custom-call | tf_op jit(solution)/shard_map/pallas_call | solution.py:529
  48.9 1.3 %copy.12 = f32[1,4,5,64]{3,1,2,0:T(4,128)} copy(f32[1,4,5,64]{3,1,2,0:T(4,128)} %bitcast.10) | data formatting | bytes 10240

commit v3 on v1

--- a/solution.py
+++ b/solution.py
@@ -90,16 +90,22 @@
 
 def kernel(
     sizes,
+    step_hbm,
+    latents_hbm,
+    fresh_hbm,
+    w_in_hbm,
+    w_out_hbm,
+    conv_first_hbm,
+    conv_second_hbm,
+    w_time_hbm,
+    temporal_hbm,
+    out_ref,
+    late_ref,
     step_ref,
     latents_ref,
     fresh_ref,
     w_in_ref,
     w_out_ref,
-    conv_first_hbm,
-    conv_second_hbm,
-    w_time_hbm,
-    temporal_hbm,
-    out_ref,
     raw_first,
     raw_second,
     raw_time,
@@ -139,6 +145,11 @@
         pltpu.make_async_copy(source, target, load_sem.at[i])
         for i, (source, target) in enumerate(
             (
+                (latents_hbm, latents_ref),
+                (fresh_hbm, fresh_ref),
+                (step_hbm, step_ref),
+                (w_in_hbm, w_in_ref),
+                (w_out_hbm, w_out_ref),
                 (conv_first_hbm, raw_first),
                 (w_time_hbm, raw_time),
                 (temporal_hbm, raw_temporal),
@@ -146,14 +157,9 @@
             )
         )
     ]
-    loads[0].start()
-    loads[1].start()
-
-    lat = latents_ref.shape[1]
-    pack_ref[...] = jnp.zeros_like(pack_ref)
-    for r in range(latents_ref.shape[0]):
-        pack_ref[0:lat, r * width : (r + 1) * width] = latents_ref[r]
-        pack_ref[8 : 8 + lat, r * width : (r + 1) * width] = fresh_ref[r]
+    for load in loads[:7]:
+        load.start()
+
     recv_frame[...] = jnp.zeros_like(recv_frame)
     recv_tap[...] = jnp.zeros_like(recv_tap)
     recv_last[...] = jnp.zeros_like(recv_last)
@@ -174,6 +180,16 @@
     pl.when(has_down)(lambda: greet({"level": level - 1}))
     pl.when(has_two_down)(lambda: greet({"level": level - 2}))
     pl.when(has_up)(lambda: greet({"level": level + 1}))
+    lat = latents_ref.shape[1]
+    pack_ref[...] = jnp.zeros_like(pack_ref)
+    loads[0].wait()
+    loads[1].wait()
+    for r in range(latents_ref.shape[0]):
+        pack_ref[0:lat, r * width : (r + 1) * width] = latents_ref[r]
+        pack_ref[8 : 8 + lat, r * width : (r + 1) * width] = fresh_ref[r]
+    loads[7].start()
+    loads[8].start()
+
     expected = n_band - 1
     for there in (has_up, has_two_up, has_down):
         expected = expected + jnp.where(there, 1, 0)
@@ -192,6 +208,8 @@
     for i in range(n_band - 1):
         band_copy(i).start()
 
+    for load in loads[2:5]:
+        load.wait()
     spare = jnp.zeros((8 - lat, channels), F32)
     w_in = jnp.concatenate([w_in_ref[...], spare], axis=0)
     w_out = jnp.concatenate([w_out_ref[...], spare], axis=0)
@@ -215,16 +233,25 @@
     angle = step.astype(F32) * frequency
     harmonic = jnp.where(lane < half_width, jnp.cos(angle), jnp.sin(angle))
 
-    loads[0].wait()
-    loads[2].start()
-    loads[3].start()
+    loads[5].wait()
     for n in range(4):
         pack_weights(n, raw_first, first_high, first_low, channels)
-    loads[1].wait()
+    loads[6].wait()
     embedded = silu(dot3(harmonic, raw_time[...]))[0:1, :]
     w_out_high, w_out_low = split(
         jnp.concatenate([w_out, jnp.zeros((24, channels), F32)], axis=0)
     )
+
+    loads[7].wait()
+    folded = jnp.concatenate(
+        [dot3(w_out, raw_temporal[k], NT) for k in range(3)]
+        + [jnp.zeros((8, channels), F32)],
+        axis=0,
+    )
+    folded_high, folded_low = split(folded)
+    loads[8].wait()
+    for n in range(4):
+        pack_weights(n, raw_second, second_high, second_low, channels)
 
     border = jnp.zeros((width, 1024), BF16)
     for ref in (act_high, act_low):
@@ -383,33 +410,22 @@
         fill_act(value_ref, norm_terms(value_ref))
         convolve(second_high, second_low, lambda place: lifted_ref[place, :])
 
-    def prepare_later():
-        for n in range(4):
-            pack_weights(n, raw_second, second_high, second_low, channels)
-
-    loads[2].wait()
-    loads[3].wait()
-    folded = jnp.concatenate(
-        [dot3(w_out, raw_temporal[k], NT) for k in range(3)]
-        + [jnp.zeros((8, channels), F32)],
-        axis=0,
-    )
-    folded_high, folded_low = split(folded)
-    run_block(frame, prepare_later)
+    run_block(frame)
     hidden = value_ref[...]
     straight = project(w_out_high, w_out_low, hidden)[0:8]
     center, factor = norm_terms(value_ref)
     taps = project(folded_high, folded_low, silu((hidden - center) * factor))
-    send_frame[0:8, :] = scale_x * frame + scale_noise * (straight + taps[8:16])
-    send_frame[8:16, :] = jnp.broadcast_to(scale_noise, (8, pixels))
-    send_tap[...] = taps[0:8]
+    send_tap[...] = taps[0:4]
     frame_copy = level_copy(0, send_frame, recv_frame, level + 1)
     tap_copy = level_copy(1, send_tap, recv_tap, level + 2)
     pl.when(has_two_up)(lambda: tap_copy.start())
+    send_frame[0:4, :] = (scale_x * frame + scale_noise * (straight + taps[8:16]))[0:4]
+    send_frame[4:8, :] = jnp.broadcast_to(scale_noise, (4, pixels))
     pl.when(has_up)(lambda: frame_copy.start())
     pl.when(has_two_down)(lambda: tap_copy.wait_recv())
     pl.when(has_down)(lambda: frame_copy.wait_recv())
-    moved = recv_frame[0:8, :] + recv_frame[8:16, :] * (recv_tap[...] + taps[16:24])
+    moved = recv_frame[0:4, :] + recv_frame[4:8, :] * (recv_tap[...] + taps[16:20])
+    moved = jnp.concatenate([moved, jnp.zeros((4, pixels), F32)], axis=0)
     frame = jnp.where(level == 0, entering, moved)
     pl.when(has_two_up)(lambda: tap_copy.wait_send())
     pl.when(has_up)(lambda: frame_copy.wait_send())
@@ -419,8 +435,8 @@
     straight = project(w_out_high, w_out_low, hidden)[0:8]
     center, factor = norm_terms(value_ref)
     taps = project(folded_high, folded_low, silu((hidden - center) * factor))
-    send_last[0] = taps[0:8]
-    send_last[1] = taps[16:24]
+    send_last[0] = taps[0:4]
+    send_last[1] = taps[16:20]
     up_copy = level_copy(2, send_last.at[0], recv_last.at[0], level + 1)
     down_copy = level_copy(3, send_last.at[1], recv_last.at[1], level - 1)
     pl.when(has_up)(lambda: up_copy.start())
@@ -429,11 +445,14 @@
     mine = frame[:, 0:held]
     for j in range(1, n_band):
         mine = jnp.where(band == j, frame[:, j * held : (j + 1) * held], mine)
+    done = scale_x * mine + scale_noise * local
+    for r in range(out_ref.shape[0]):
+        out_ref[r] = done[0:lat, r * width : (r + 1) * width]
     pl.when(has_down)(lambda: up_copy.wait_recv())
     pl.when(has_up)(lambda: down_copy.wait_recv())
-    done = scale_x * mine + scale_noise * (local + recv_last[0] + recv_last[1])
+    late = scale_noise * (recv_last[0] + recv_last[1])
     for r in range(out_ref.shape[0]):
-        out_ref[r] = done[0:lat, r * width : (r + 1) * width]
+        late_ref[r] = late[0:lat, r * width : (r + 1) * width]
     pl.when(has_up)(lambda: up_copy.wait_send())
     pl.when(has_down)(lambda: down_copy.wait_send())
 
@@ -452,12 +471,15 @@
     vmem = pl.BlockSpec(memory_space=pltpu.VMEM)
     hbm = pl.BlockSpec(memory_space=pl.ANY)
     sem = pltpu.SemaphoreType.DMA
-    result = pl.pallas_call(
+    ready, late = pl.pallas_call(
         functools.partial(kernel, (n_level, n_band, channels, height, width, chunk)),
-        out_shape=jax.ShapeDtypeStruct((band_rows, lat, width), F32),
-        in_specs=[pl.BlockSpec(memory_space=pltpu.SMEM)] + [vmem] * 4 + [hbm] * 4,
-        out_specs=vmem,
+        out_shape=[jax.ShapeDtypeStruct((band_rows, lat, width), F32)] * 2,
+        in_specs=[hbm] * 9,
+        out_specs=[vmem] * 2,
         scratch_shapes=[
+            pltpu.SMEM((1,), jnp.int32),
+            *[pltpu.VMEM((band_rows, lat, width), F32)] * 2,
+            *[pltpu.VMEM((lat, channels), F32)] * 2,
             pltpu.VMEM(conv_first.shape, F32),
             pltpu.VMEM(conv_second.shape, F32),
             pltpu.VMEM(w_time.shape, F32),
@@ -468,10 +490,10 @@
             pltpu.VMEM((pixels + 2 * width, 256), F32),
             pltpu.VMEM((16, held), F32),
             pltpu.VMEM((max(n_band - 1, 1), 16, held), F32),
-            *[pltpu.VMEM((16, pixels), F32)] * 2,
             *[pltpu.VMEM((8, pixels), F32)] * 2,
-            *[pltpu.VMEM((2, 8, held), F32)] * 2,
-            sem((4,)),
+            *[pltpu.VMEM((4, pixels), F32)] * 2,
+            *[pltpu.VMEM((2, 4, held), F32)] * 2,
+            sem((9,)),
             sem((max(n_band - 1, 1),)),
             sem((max(n_band - 1, 1),)),
             sem((4,)),
@@ -491,7 +513,7 @@
         w_time,
         temporal,
     )
-    return result.transpose(1, 0, 2)[None]
+    return (ready + late).transpose(1, 0, 2)[None]
 
 
 def solution(mesh):

time: 38.5 us -> 37.1 us (0.964)
  Pallas kernels: 36.2 us -> 34.8 us
  other arithmetic: 0 us -> 1.32 us
  local copies, waits for them, and re-layouts: 1.3 us -> 0 us
    pallas_call x1, Pallas kernels: 36.2 us -> 34.8 us  [on_device(): pl.pallas_call(functools.partial(kernel, (n_level, n_band, channels, heig...]
    broadcast_in_dim x0 -> x1, other arithmetic: none -> 1.32 us  [on_device(): return (ready + late).transpose(1, 0, 2)[None]]
    unnamed x1 -> x0, local copies, waits for them, and re-layouts: 1.3 us -> none
where the time goes in v3:
time: 37.1 us; the launch traced here: 36.8 us
  Pallas kernels  34.8 us (94%)
  other arithmetic  1.32 us (4%)
  between operations  0.66 us (2%)
    pallas_call x1, Pallas kernels, on_device(): pl.pallas_call(functools.partial(kernel, (n_level, n_band, channels, heig...  34.8 us
    broadcast_in_dim x1, other arithmetic, on_device(): return (ready + late).transpose(1, 0, 2)[None]  1.32 us

profile of v3, /device:TPU:23, one launch (start us, length us, event | category | flops | bytes accessed | tf_op | source)
XLA Modules:
  0.0 36.8 jit_solution(3030091316338931361)
XLA Ops:
  0.7 34.8 %shard_map.91 = (f32[5,4,64]{2,1,0:T(4,128)}, f32[5,4,64]{2,1,0:T(4,128)}) custom-call(s32[1]{0:T(128)S(6)} %copy.10.step_hbm, f32[5,4,64]{2,1,0:T(4,128)} %bitcast.11, f32[5,4,64]{2,1,0:T(4,128)} %bitcast.12, f32[4,320]{1,0:T(4,128)} %w_in_hbm.1, f32[4,320]{1,0:T(4,128)} %bitcast.13, f32[3,3,320,320]{3,2,1,0:T(8,128)} %conv_first_hbm.1, ...), custom_call_target="tpu_custom_call" | custom-call | tf_op jit(solution)/shard_map/pallas_call | solution.py:474
  35.5 1.3 %add_bitcast_fusion = f32[1,4,5,64]{3,1,2,0:T(4,128)} fusion(f32[5,4,64]{2,1,0:T(4,128)} %get-tuple-element.7, f32[5,4,64]{2,1,0:T(4,128)} %get-tuple-element.8), kind=kLoop, calls=%fused_computation | loop fusion | flops 1280 | bytes 15360 | tf_op jit(solution)/shard_map/broadcast_in_dim | solution.py:516
